TPU v7x, 128 devices: a whole 4x4x4 slice. The times are simulated.
128 devices in a mesh: clus: 128 (over y, z, x, core).
Axes of the slice: x: 4, y: 4, z: 4, core: 2. Of those that a mesh axis runs over, the one named last changes fastest.
Arguments:
- charges: float32 [32, 1048576], P(None, 'clus'), may hold values from -6 to 6
- positions: float32 [3, 1048576], P(None, 'clus'), may hold values from -2 to 2
- quad_weights: float32 [1048576], P('clus'), may hold values from 0.1 to 1
- leaf_basis: float32 [4096, 64, 256], P('clus'), may hold values from -0.375 to 0.375
- leaf_nodes: float32 [3, 262144], P(None, 'clus'), may hold values from -2 to 2
- leaf_transfer: float32 [64, 262144], P(None, 'clus'), may hold values from -0.75 to 0.75
- mid_nodes: float32 [3, 8192], P(None, 'clus'), may hold values from -2 to 2
- mid_transfer: float32 [64, 8192], P(None, 'clus'), may hold values from -0.75 to 0.75
- top_nodes: float32 [3, 1024], replicated, may hold values from -2 to 2
- near_list: int32 [4096, 27], P('clus'), may hold values from 0 to 4095, as said below
- near_count: int32 [4096], P('clus'), may hold values from 1 to 27, as said below
- far_list: int32 [4096, 16], P('clus'), may hold values from 0 to 4095, as said below
- mid_mask: int32 [128, 128], P('clus'), may hold values 0 or 1
- top_mask: int32 [16, 16], replicated, may hold values 0 or 1
Outputs:
- potential: float32 [32, 1048576], P(None, 'clus')
Inputs may be any that keep to these rules, and one draw needn't show every extreme that they name: `near_list`: every entry names a leaf of the device that owns the row's leaf or of the device just before or after it in a cycle over devices (the last device's next one being the first); the entries of one row are distinct and differ from those of the row's far_list. `far_list`: the same locality holds: sources lie on the owning device or its two cyclic neighbours; entries of one row are distinct. `near_count`: some leaf has all 27 slots live in every draw.
All inputs are finite; a program needn't handle non-finite values. No bound on the sum of `mid_mask` on one device may be relied on, other than what follows from the above.
Results may differ from a plain program's by a relative error of at most 0.0003.
Values sent between devices are 32-bit elements; how exact they have to be, the bound alone decides.
No kernel may reach another device: no remote copies, remote signals or barrier semaphores. Data moves between devices by JAX's collectives and lax.ppermute only.
A program may use at most 128 MiB of HBM per device.

v0:
```python
import math

import jax
import jax.numpy as jnp
from jax import lax
from jax.sharding import PartitionSpec as P

LEAF = 256
RANK = 64
NRHS = 32
LEAF_DEV = 32
NEAR_MAX = 27
GROUP = 8


smoothing = 0.05
inv_four_pi = 1.0 / (4.0 * math.pi)
highest = lax.Precision.HIGHEST


def extended(array, sides, width):
    for axis, dim in sides:
        size, length = (lax.axis_size(axis), array.shape[dim])
        up = [(i, (i + 1) % size) for i in range(size)]
        down = [(j, i) for i, j in up]
        last = lax.slice_in_dim(array, length - width, length, axis=dim)
        first = lax.slice_in_dim(array, 0, width, axis=dim)
        before = lax.ppermute(last, axis, up)
        after = lax.ppermute(first, axis, down)
        array = jnp.concatenate([before, array, after], axis=dim)
    return array


def green(source, target):
    first = source[0][..., :, None] - target[0][..., None, :]
    second = source[1][..., :, None] - target[1][..., None, :]
    third = source[2][..., :, None] - target[2][..., None, :]
    total = first * first + second * second + third * third
    return inv_four_pi / jnp.sqrt(total + smoothing * smoothing)


def shards(
    charges,
    positions,
    quad_weights,
    leaf_basis,
    leaf_nodes,
    leaf_transfer,
    mid_nodes,
    mid_transfer,
    top_nodes,
    near_list,
    near_count,
    far_list,
    mid_mask,
    top_mask,
):
    devices = lax.axis_size("clus")
    myself = lax.axis_index("clus")
    all_leaves = LEAF_DEV * devices
    top_count = devices // GROUP
    point_pack = jnp.concatenate([charges, positions, quad_weights[None, :]], axis=0)
    leaf_charges = charges.reshape(NRHS, LEAF_DEV, LEAF)
    leaf_coef = jnp.einsum("rlb,lkb->rlk", leaf_charges, leaf_basis, precision=highest)
    coef_flat = leaf_coef.reshape(NRHS, LEAF_DEV * RANK)
    coef_pack = jnp.concatenate([coef_flat, leaf_nodes], axis=0)
    point_wide = extended(point_pack, (("clus", 1),), LEAF_DEV * LEAF)
    coef_wide = extended(coef_pack, (("clus", 1),), LEAF_DEV * RANK)
    contract_last = (((1,), (1,)), ((), ()))
    mid_coef = lax.dot_general(coef_flat, leaf_transfer, contract_last, precision=highest)
    upward = lax.dot_general(mid_coef, mid_transfer, contract_last, precision=highest)
    level_pack = jnp.concatenate([mid_coef, mid_nodes], axis=0)
    everyone = lax.all_gather(level_pack, "clus", axis=1, tiled=True)
    all_coef = everyone[:NRHS]
    all_nodes = everyone[NRHS : NRHS + 3]
    parent = myself // GROUP
    selector = (jnp.arange(top_count) == parent).astype(jnp.float32)
    placed = (selector[None, :, None] * upward[:, None, :]).reshape(NRHS, top_count * RANK)
    top_coef = lax.psum(placed, "clus")
    top_target = lax.dynamic_slice_in_dim(top_nodes, parent * RANK, RANK, 1)
    top_row = lax.dynamic_index_in_dim(top_mask, parent, 0, keepdims=False)
    top_select = jnp.repeat(top_row.astype(jnp.float32), RANK)[:, None]
    top_field = jnp.dot(top_coef, green(top_nodes, top_target) * top_select, precision=highest)
    mid_select = jnp.repeat(mid_mask[0].astype(jnp.float32), RANK)[:, None]
    mid_field = jnp.dot(all_coef, green(all_nodes, mid_nodes) * mid_select, precision=highest)
    mid_field = mid_field + jnp.dot(top_field, mid_transfer, precision=highest)
    leaf_down = jnp.dot(mid_field, leaf_transfer, precision=highest).reshape(NRHS, LEAF_DEV, RANK)
    first_leaf = myself * LEAF_DEV - LEAF_DEV
    coef_window = coef_wide.reshape(NRHS + 3, 3 * LEAF_DEV, RANK)
    far_local = (far_list - first_leaf) % all_leaves
    far_picked = jnp.take(coef_window, far_local, axis=1)
    target_nodes = leaf_nodes.reshape(3, LEAF_DEV, RANK)
    coupling = green(far_picked[NRHS:], target_nodes[:, :, None, :])
    leaf_field = (
        jnp.einsum("rlfj,lfji->rli", far_picked[:NRHS], coupling, precision=highest) + leaf_down
    )
    far_out = jnp.einsum("rlk,lkb->rlb", leaf_field, leaf_basis, precision=highest)
    point_window = point_wide.reshape(NRHS + 4, 3 * LEAF_DEV, LEAF)
    near_local = (near_list - first_leaf) % all_leaves
    target_points = positions.reshape(3, LEAF_DEV, LEAF)
    empty = jnp.zeros((NRHS, LEAF_DEV, LEAF), jnp.float32)

    def slot(index, total):
        chosen = lax.dynamic_index_in_dim(near_local, index, 1, keepdims=False)
        live = (index < near_count).astype(jnp.float32)
        picked = jnp.take(point_window, chosen, axis=1)
        weighted = picked[NRHS + 3] * live[:, None]
        block_kernel = green(picked[NRHS : NRHS + 3], target_points) * weighted[:, :, None]
        return total + jnp.einsum("rlb,lba->rla", picked[:NRHS], block_kernel, precision=highest)

    near_out = lax.fori_loop(0, NEAR_MAX, slot, empty)
    return (far_out + near_out).reshape(NRHS, LEAF_DEV * LEAF)


def solution(mesh):
    in_specs = (
        P(None, "clus"),
        P(None, "clus"),
        P("clus"),
        P("clus", None, None),
        P(None, "clus"),
        P(None, "clus"),
        P(None, "clus"),
        P(None, "clus"),
        P(),
        P("clus", None),
        P("clus"),
        P("clus", None),
        P("clus", None),
        P(),
    )
    out_specs = P(None, "clus")
    return jax.shard_map(shards, mesh=mesh, in_specs=in_specs, out_specs=out_specs, check_vma=False)
```

profile of v0, /device:TPU:1, one launch (start us, length us, event | category | flops | bytes accessed | tf_op | source)
XLA Modules:
  0.0 715.4 jit_solution(12227380253784975760)
XLA Ops:
  22.0 5.3 collective-permute-start.3
  44.0 128.2 %all-reduce.2.cloned.1.call-done = f32[32,1024]{1,0:T(8,128)} async-done(((f32[32,1024]{1,0:T(8,128)}), f32[32,1024]{1,0:T(8,128)}) %all-reduce.2.cloned.1.call-update) | async-done | bytes 131088 | tf_op jit(solution)/shard_map/psum | solution.py:79
  183.2 6.8 gather_fusion.1
  206.9 460.8 %while.14 = (s32[]{:T(128)}, f32[32,32,256]{2,0,1:T(8,128)}, s32[32,27]{0,1:T(8,128)S(1)}, f32[36,96,256]{2,0,1:T(8,128)}, f32[3,32,256]{2,1,0:T(8,128)S(1)}, /*index=5*/s32[32]{0:T(128)}, s32[]{:T(128)}, s32[]{:T(128)}) while((s32[]{:T(128)}, f32[32,32,256]{2,0,1:T(8,128)}, s32[32,27]{0,1:T(8,128)S(1)}, f32[36,96,256]{2,0,1:T(8,128)}, ...), condition=%wide.region_2.3_spmd.clone, body=%wide.region_1.2_spmd.clone.sunk | while | flops 827114752 | bytes 13566075 | solution.py:111
  212.3 11.5 %fusion.145 = f32[32,32,256]{2,0,1:T(8,128)} fusion(f32[32,256]{1,0:T(8,128)S(1)} %fusion.144, f32[32,256]{1,0:T(8,128)S(1)} %get-tuple-element.263, f32[32,256]{1,0:T(8,128)S(1)} %get-tuple-element.266, f32[32,256]{1,0:T(8,128)S(1)} %get-tuple-element.267, f32[32,256]{1,0:T(8,128)S(1)} %get-tuple-element.268, ...), kind=kOutput, calls=%fused_computation.23.clone.1 | convolution fusion | flops 826802176 | bytes 3375105 | tf_op jit(solution)/shard_map/while/body/eval_jaxpr/rlb,lba->rla/dot_general | solution.py:109
  229.3 11.6 %fusion.145 = f32[32,32,256]{2,0,1:T(8,128)} fusion(f32[32,256]{1,0:T(8,128)S(1)} %fusion.144, f32[32,256]{1,0:T(8,128)S(1)} %get-tuple-element.263, f32[32,256]{1,0:T(8,128)S(1)} %get-tuple-element.266, f32[32,256]{1,0:T(8,128)S(1)} %get-tuple-element.267, f32[32,256]{1,0:T(8,128)S(1)} %get-tuple-element.268, ...), kind=kOutput, calls=%fused_computation.23.clone.1 | convolution fusion | flops 826802176 | bytes 3375105 | tf_op jit(solution)/shard_map/while/body/eval_jaxpr/rlb,lba->rla/dot_general | solution.py:109
  246.4 11.6 %fusion.145 = f32[32,32,256]{2,0,1:T(8,128)} fusion(f32[32,256]{1,0:T(8,128)S(1)} %fusion.144, f32[32,256]{1,0:T(8,128)S(1)} %get-tuple-element.263, f32[32,256]{1,0:T(8,128)S(1)} %get-tuple-element.266, f32[32,256]{1,0:T(8,128)S(1)} %get-tuple-element.267, f32[32,256]{1,0:T(8,128)S(1)} %get-tuple-element.268, ...), kind=kOutput, calls=%fused_computation.23.clone.1 | convolution fusion | flops 826802176 | bytes 3375105 | tf_op jit(solution)/shard_map/while/body/eval_jaxpr/rlb,lba->rla/dot_general | solution.py:109
  263.5 11.6 %fusion.145 = f32[32,32,256]{2,0,1:T(8,128)} fusion(f32[32,256]{1,0:T(8,128)S(1)} %fusion.144, f32[32,256]{1,0:T(8,128)S(1)} %get-tuple-element.263, f32[32,256]{1,0:T(8,128)S(1)} %get-tuple-element.266, f32[32,256]{1,0:T(8,128)S(1)} %get-tuple-element.267, f32[32,256]{1,0:T(8,128)S(1)} %get-tuple-element.268, ...), kind=kOutput, calls=%fused_computation.23.clone.1 | convolution fusion | flops 826802176 | bytes 3375105 | tf_op jit(solution)/shard_map/while/body/eval_jaxpr/rlb,lba->rla/dot_general | solution.py:109
  280.5 11.6 %fusion.145 = f32[32,32,256]{2,0,1:T(8,128)} fusion(f32[32,256]{1,0:T(8,128)S(1)} %fusion.144, f32[32,256]{1,0:T(8,128)S(1)} %get-tuple-element.263, f32[32,256]{1,0:T(8,128)S(1)} %get-tuple-element.266, f32[32,256]{1,0:T(8,128)S(1)} %get-tuple-element.267, f32[32,256]{1,0:T(8,128)S(1)} %get-tuple-element.268, ...), kind=kOutput, calls=%fused_computation.23.clone.1 | convolution fusion | flops 826802176 | bytes 3375105 | tf_op jit(solution)/shard_map/while/body/eval_jaxpr/rlb,lba->rla/dot_general | solution.py:109
  297.6 11.6 %fusion.145 = f32[32,32,256]{2,0,1:T(8,128)} fusion(f32[32,256]{1,0:T(8,128)S(1)} %fusion.144, f32[32,256]{1,0:T(8,128)S(1)} %get-tuple-element.263, f32[32,256]{1,0:T(8,128)S(1)} %get-tuple-element.266, f32[32,256]{1,0:T(8,128)S(1)} %get-tuple-element.267, f32[32,256]{1,0:T(8,128)S(1)} %get-tuple-element.268, ...), kind=kOutput, calls=%fused_computation.23.clone.1 | convolution fusion | flops 826802176 | bytes 3375105 | tf_op jit(solution)/shard_map/while/body/eval_jaxpr/rlb,lba->rla/dot_general | solution.py:109
  314.7 11.6 %fusion.145 = f32[32,32,256]{2,0,1:T(8,128)} fusion(f32[32,256]{1,0:T(8,128)S(1)} %fusion.144, f32[32,256]{1,0:T(8,128)S(1)} %get-tuple-element.263, f32[32,256]{1,0:T(8,128)S(1)} %get-tuple-element.266, f32[32,256]{1,0:T(8,128)S(1)} %get-tuple-element.267, f32[32,256]{1,0:T(8,128)S(1)} %get-tuple-element.268, ...), kind=kOutput, calls=%fused_computation.23.clone.1 | convolution fusion | flops 826802176 | bytes 3375105 | tf_op jit(solution)/shard_map/while/body/eval_jaxpr/rlb,lba->rla/dot_general | solution.py:109
  331.7 11.6 %fusion.145 = f32[32,32,256]{2,0,1:T(8,128)} fusion(f32[32,256]{1,0:T(8,128)S(1)} %fusion.144, f32[32,256]{1,0:T(8,128)S(1)} %get-tuple-element.263, f32[32,256]{1,0:T(8,128)S(1)} %get-tuple-element.266, f32[32,256]{1,0:T(8,128)S(1)} %get-tuple-element.267, f32[32,256]{1,0:T(8,128)S(1)} %get-tuple-element.268, ...), kind=kOutput, calls=%fused_computation.23.clone.1 | convolution fusion | flops 826802176 | bytes 3375105 | tf_op jit(solution)/shard_map/while/body/eval_jaxpr/rlb,lba->rla/dot_general | solution.py:109
  348.8 11.6 %fusion.145 = f32[32,32,256]{2,0,1:T(8,128)} fusion(f32[32,256]{1,0:T(8,128)S(1)} %fusion.144, f32[32,256]{1,0:T(8,128)S(1)} %get-tuple-element.263, f32[32,256]{1,0:T(8,128)S(1)} %get-tuple-element.266, f32[32,256]{1,0:T(8,128)S(1)} %get-tuple-element.267, f32[32,256]{1,0:T(8,128)S(1)} %get-tuple-element.268, ...), kind=kOutput, calls=%fused_computation.23.clone.1 | convolution fusion | flops 826802176 | bytes 3375105 | tf_op jit(solution)/shard_map/while/body/eval_jaxpr/rlb,lba->rla/dot_general | solution.py:109
  365.9 11.6 %fusion.145 = f32[32,32,256]{2,0,1:T(8,128)} fusion(f32[32,256]{1,0:T(8,128)S(1)} %fusion.144, f32[32,256]{1,0:T(8,128)S(1)} %get-tuple-element.263, f32[32,256]{1,0:T(8,128)S(1)} %get-tuple-element.266, f32[32,256]{1,0:T(8,128)S(1)} %get-tuple-element.267, f32[32,256]{1,0:T(8,128)S(1)} %get-tuple-element.268, ...), kind=kOutput, calls=%fused_computation.23.clone.1 | convolution fusion | flops 826802176 | bytes 3375105 | tf_op jit(solution)/shard_map/while/body/eval_jaxpr/rlb,lba->rla/dot_general | solution.py:109
  383.0 11.6 %fusion.145 = f32[32,32,256]{2,0,1:T(8,128)} fusion(f32[32,256]{1,0:T(8,128)S(1)} %fusion.144, f32[32,256]{1,0:T(8,128)S(1)} %get-tuple-element.263, f32[32,256]{1,0:T(8,128)S(1)} %get-tuple-element.266, f32[32,256]{1,0:T(8,128)S(1)} %get-tuple-element.267, f32[32,256]{1,0:T(8,128)S(1)} %get-tuple-element.268, ...), kind=kOutput, calls=%fused_computation.23.clone.1 | convolution fusion | flops 826802176 | bytes 3375105 | tf_op jit(solution)/shard_map/while/body/eval_jaxpr/rlb,lba->rla/dot_general | solution.py:109
  400.0 11.6 %fusion.145 = f32[32,32,256]{2,0,1:T(8,128)} fusion(f32[32,256]{1,0:T(8,128)S(1)} %fusion.144, f32[32,256]{1,0:T(8,128)S(1)} %get-tuple-element.263, f32[32,256]{1,0:T(8,128)S(1)} %get-tuple-element.266, f32[32,256]{1,0:T(8,128)S(1)} %get-tuple-element.267, f32[32,256]{1,0:T(8,128)S(1)} %get-tuple-element.268, ...), kind=kOutput, calls=%fused_computation.23.clone.1 | convolution fusion | flops 826802176 | bytes 3375105 | tf_op jit(solution)/shard_map/while/body/eval_jaxpr/rlb,lba->rla/dot_general | solution.py:109
  417.1 11.6 %fusion.145 = f32[32,32,256]{2,0,1:T(8,128)} fusion(f32[32,256]{1,0:T(8,128)S(1)} %fusion.144, f32[32,256]{1,0:T(8,128)S(1)} %get-tuple-element.263, f32[32,256]{1,0:T(8,128)S(1)} %get-tuple-element.266, f32[32,256]{1,0:T(8,128)S(1)} %get-tuple-element.267, f32[32,256]{1,0:T(8,128)S(1)} %get-tuple-element.268, ...), kind=kOutput, calls=%fused_computation.23.clone.1 | convolution fusion | flops 826802176 | bytes 3375105 | tf_op jit(solution)/shard_map/while/body/eval_jaxpr/rlb,lba->rla/dot_general | solution.py:109
  434.2 11.6 %fusion.145 = f32[32,32,256]{2,0,1:T(8,128)} fusion(f32[32,256]{1,0:T(8,128)S(1)} %fusion.144, f32[32,256]{1,0:T(8,128)S(1)} %get-tuple-element.263, f32[32,256]{1,0:T(8,128)S(1)} %get-tuple-element.266, f32[32,256]{1,0:T(8,128)S(1)} %get-tuple-element.267, f32[32,256]{1,0:T(8,128)S(1)} %get-tuple-element.268, ...), kind=kOutput, calls=%fused_computation.23.clone.1 | convolution fusion | flops 826802176 | bytes 3375105 | tf_op jit(solution)/shard_map/while/body/eval_jaxpr/rlb,lba->rla/dot_general | solution.py:109
  451.2 11.6 %fusion.145 = f32[32,32,256]{2,0,1:T(8,128)} fusion(f32[32,256]{1,0:T(8,128)S(1)} %fusion.144, f32[32,256]{1,0:T(8,128)S(1)} %get-tuple-element.263, f32[32,256]{1,0:T(8,128)S(1)} %get-tuple-element.266, f32[32,256]{1,0:T(8,128)S(1)} %get-tuple-element.267, f32[32,256]{1,0:T(8,128)S(1)} %get-tuple-element.268, ...), kind=kOutput, calls=%fused_computation.23.clone.1 | convolution fusion | flops 826802176 | bytes 3375105 | tf_op jit(solution)/shard_map/while/body/eval_jaxpr/rlb,lba->rla/dot_general | solution.py:109
  468.3 11.6 %fusion.145 = f32[32,32,256]{2,0,1:T(8,128)} fusion(f32[32,256]{1,0:T(8,128)S(1)} %fusion.144, f32[32,256]{1,0:T(8,128)S(1)} %get-tuple-element.263, f32[32,256]{1,0:T(8,128)S(1)} %get-tuple-element.266, f32[32,256]{1,0:T(8,128)S(1)} %get-tuple-element.267, f32[32,256]{1,0:T(8,128)S(1)} %get-tuple-element.268, ...), kind=kOutput, calls=%fused_computation.23.clone.1 | convolution fusion | flops 826802176 | bytes 3375105 | tf_op jit(solution)/shard_map/while/body/eval_jaxpr/rlb,lba->rla/dot_general | solution.py:109
  485.4 11.6 %fusion.145 = f32[32,32,256]{2,0,1:T(8,128)} fusion(f32[32,256]{1,0:T(8,128)S(1)} %fusion.144, f32[32,256]{1,0:T(8,128)S(1)} %get-tuple-element.263, f32[32,256]{1,0:T(8,128)S(1)} %get-tuple-element.266, f32[32,256]{1,0:T(8,128)S(1)} %get-tuple-element.267, f32[32,256]{1,0:T(8,128)S(1)} %get-tuple-element.268, ...), kind=kOutput, calls=%fused_computation.23.clone.1 | convolution fusion | flops 826802176 | bytes 3375105 | tf_op jit(solution)/shard_map/while/body/eval_jaxpr/rlb,lba->rla/dot_general | solution.py:109
  502.4 11.6 %fusion.145 = f32[32,32,256]{2,0,1:T(8,128)} fusion(f32[32,256]{1,0:T(8,128)S(1)} %fusion.144, f32[32,256]{1,0:T(8,128)S(1)} %get-tuple-element.263, f32[32,256]{1,0:T(8,128)S(1)} %get-tuple-element.266, f32[32,256]{1,0:T(8,128)S(1)} %get-tuple-element.267, f32[32,256]{1,0:T(8,128)S(1)} %get-tuple-element.268, ...), kind=kOutput, calls=%fused_computation.23.clone.1 | convolution fusion | flops 826802176 | bytes 3375105 | tf_op jit(solution)/shard_map/while/body/eval_jaxpr/rlb,lba->rla/dot_general | solution.py:109
  519.5 11.6 %fusion.145 = f32[32,32,256]{2,0,1:T(8,128)} fusion(f32[32,256]{1,0:T(8,128)S(1)} %fusion.144, f32[32,256]{1,0:T(8,128)S(1)} %get-tuple-element.263, f32[32,256]{1,0:T(8,128)S(1)} %get-tuple-element.266, f32[32,256]{1,0:T(8,128)S(1)} %get-tuple-element.267, f32[32,256]{1,0:T(8,128)S(1)} %get-tuple-element.268, ...), kind=kOutput, calls=%fused_computation.23.clone.1 | convolution fusion | flops 826802176 | bytes 3375105 | tf_op jit(solution)/shard_map/while/body/eval_jaxpr/rlb,lba->rla/dot_general | solution.py:109
  536.6 11.6 %fusion.145 = f32[32,32,256]{2,0,1:T(8,128)} fusion(f32[32,256]{1,0:T(8,128)S(1)} %fusion.144, f32[32,256]{1,0:T(8,128)S(1)} %get-tuple-element.263, f32[32,256]{1,0:T(8,128)S(1)} %get-tuple-element.266, f32[32,256]{1,0:T(8,128)S(1)} %get-tuple-element.267, f32[32,256]{1,0:T(8,128)S(1)} %get-tuple-element.268, ...), kind=kOutput, calls=%fused_computation.23.clone.1 | convolution fusion | flops 826802176 | bytes 3375105 | tf_op jit(solution)/shard_map/while/body/eval_jaxpr/rlb,lba->rla/dot_general | solution.py:109
  553.6 11.6 %fusion.145 = f32[32,32,256]{2,0,1:T(8,128)} fusion(f32[32,256]{1,0:T(8,128)S(1)} %fusion.144, f32[32,256]{1,0:T(8,128)S(1)} %get-tuple-element.263, f32[32,256]{1,0:T(8,128)S(1)} %get-tuple-element.266, f32[32,256]{1,0:T(8,128)S(1)} %get-tuple-element.267, f32[32,256]{1,0:T(8,128)S(1)} %get-tuple-element.268, ...), kind=kOutput, calls=%fused_computation.23.clone.1 | convolution fusion | flops 826802176 | bytes 3375105 | tf_op jit(solution)/shard_map/while/body/eval_jaxpr/rlb,lba->rla/dot_general | solution.py:109
  570.7 11.6 %fusion.145 = f32[32,32,256]{2,0,1:T(8,128)} fusion(f32[32,256]{1,0:T(8,128)S(1)} %fusion.144, f32[32,256]{1,0:T(8,128)S(1)} %get-tuple-element.263, f32[32,256]{1,0:T(8,128)S(1)} %get-tuple-element.266, f32[32,256]{1,0:T(8,128)S(1)} %get-tuple-element.267, f32[32,256]{1,0:T(8,128)S(1)} %get-tuple-element.268, ...), kind=kOutput, calls=%fused_computation.23.clone.1 | convolution fusion | flops 826802176 | bytes 3375105 | tf_op jit(solution)/shard_map/while/body/eval_jaxpr/rlb,lba->rla/dot_general | solution.py:109
  587.8 11.6 %fusion.145 = f32[32,32,256]{2,0,1:T(8,128)} fusion(f32[32,256]{1,0:T(8,128)S(1)} %fusion.144, f32[32,256]{1,0:T(8,128)S(1)} %get-tuple-element.263, f32[32,256]{1,0:T(8,128)S(1)} %get-tuple-element.266, f32[32,256]{1,0:T(8,128)S(1)} %get-tuple-element.267, f32[32,256]{1,0:T(8,128)S(1)} %get-tuple-element.268, ...), kind=kOutput, calls=%fused_computation.23.clone.1 | convolution fusion | flops 826802176 | bytes 3375105 | tf_op jit(solution)/shard_map/while/body/eval_jaxpr/rlb,lba->rla/dot_general | solution.py:109
  604.9 11.6 %fusion.145 = f32[32,32,256]{2,0,1:T(8,128)} fusion(f32[32,256]{1,0:T(8,128)S(1)} %fusion.144, f32[32,256]{1,0:T(8,128)S(1)} %get-tuple-element.263, f32[32,256]{1,0:T(8,128)S(1)} %get-tuple-element.266, f32[32,256]{1,0:T(8,128)S(1)} %get-tuple-element.267, f32[32,256]{1,0:T(8,128)S(1)} %get-tuple-element.268, ...), kind=kOutput, calls=%fused_computation.23.clone.1 | convolution fusion | flops 826802176 | bytes 3375105 | tf_op jit(solution)/shard_map/while/body/eval_jaxpr/rlb,lba->rla/dot_general | solution.py:109
  621.9 11.6 %fusion.145 = f32[32,32,256]{2,0,1:T(8,128)} fusion(f32[32,256]{1,0:T(8,128)S(1)} %fusion.144, f32[32,256]{1,0:T(8,128)S(1)} %get-tuple-element.263, f32[32,256]{1,0:T(8,128)S(1)} %get-tuple-element.266, f32[32,256]{1,0:T(8,128)S(1)} %get-tuple-element.267, f32[32,256]{1,0:T(8,128)S(1)} %get-tuple-element.268, ...), kind=kOutput, calls=%fused_computation.23.clone.1 | convolution fusion | flops 826802176 | bytes 3375105 | tf_op jit(solution)/shard_map/while/body/eval_jaxpr/rlb,lba->rla/dot_general | solution.py:109
  639.0 11.6 %fusion.145 = f32[32,32,256]{2,0,1:T(8,128)} fusion(f32[32,256]{1,0:T(8,128)S(1)} %fusion.144, f32[32,256]{1,0:T(8,128)S(1)} %get-tuple-element.263, f32[32,256]{1,0:T(8,128)S(1)} %get-tuple-element.266, f32[32,256]{1,0:T(8,128)S(1)} %get-tuple-element.267, f32[32,256]{1,0:T(8,128)S(1)} %get-tuple-element.268, ...), kind=kOutput, calls=%fused_computation.23.clone.1 | convolution fusion | flops 826802176 | bytes 3375105 | tf_op jit(solution)/shard_map/while/body/eval_jaxpr/rlb,lba->rla/dot_general | solution.py:109
  656.1 11.6 %fusion.145 = f32[32,32,256]{2,0,1:T(8,128)} fusion(f32[32,256]{1,0:T(8,128)S(1)} %fusion.144, f32[32,256]{1,0:T(8,128)S(1)} %get-tuple-element.263, f32[32,256]{1,0:T(8,128)S(1)} %get-tuple-element.266, f32[32,256]{1,0:T(8,128)S(1)} %get-tuple-element.267, f32[32,256]{1,0:T(8,128)S(1)} %get-tuple-element.268, ...), kind=kOutput, calls=%fused_computation.23.clone.1 | convolution fusion | flops 826802176 | bytes 3375105 | tf_op jit(solution)/shard_map/while/body/eval_jaxpr/rlb,lba->rla/dot_general | solution.py:109
  677.2 29.1 %fusion.69 = f32[32,32,64]{2,0,1:T(8,128)S(1)} fusion(f32[35,32,16,64]{3,0,2,1:T(8,128)} %copy-done.2, f32[32,64]{1,0:T(8,128)} %sub.310, f32[32,16,64]{2,1,0:T(8,128)} %bitcast.127, f32[32,64]{1,0:T(8,128)} %sub.305, f32[32,16,64]{2,1,0:T(8,128)} %bitcast.128, f32[32,64]{1,0:T(8,128)} %sub.300, f32[32,16,64]{2,1,0:T(8,128)} %bitcast.126, ...), kind=kOutput, calls=%fused_computation.80 | convolution fusion | flops 826343424 | bytes 9748480 | tf_op jit(solution)/shard_map/rlfj,lfji->rli/dot_general | solution.py:95
  (496 shorter events, 217.2 us)
Async XLA Ops:
  6.5 11.8 %copy-start.3 = (f32[32,8192]{1,0:T(8,128)S(1)}, f32[32,8192]{1,0:T(8,128)}, u32[]{:S(2)}) copy-start(f32[32,8192]{1,0:T(8,128)} %param.16) | copy-start | bytes 3145732
  6.5 11.8 %copy-start.5 = (f32[3,8192]{1,0:T(4,128)S(1)}, f32[3,8192]{1,0:T(4,128)}, u32[]{:S(2)}) copy-start(f32[3,8192]{1,0:T(4,128)} %param.17) | copy-start | bytes 294916
  6.5 165.7 %all-reduce.2.cloned.1.call-start = ((), (), s32[]{:S(2)}) async-start(), calls=%async_computation | async-start | bytes 262144 | tf_op jit(solution)/shard_map/psum | solution.py:79
  15.7 158.5 %collective-permute-start = (f32[35,2048]{1,0:T(8,128)}, f32[35,2048]{1,0:T(8,128)}, u32[]{:S(2)}, u32[]{:S(2)}) collective-permute-start(f32[35,2048]{1,0:T(8,128)} %constant_dynamic-update-slice_fusion), channel_id=1, source_target_pairs={{0,1},{1,2},{2,3},{3,4},{4,5},{5,6},{6,7},{7,8},{8,9},{9,10},{10,1... | collective-permute-start | bytes 860168 | tf_op jit(solution)/shard_map/ppermute | solution.py:28
  18.3 155.9 %collective-permute-start.1 = (f32[35,2048]{1,0:T(8,128)}, f32[35,2048]{1,0:T(8,128)}, u32[]{:S(2)}, u32[]{:S(2)}) collective-permute-start(f32[35,2048]{1,0:T(8,128)} %constant_dynamic-update-slice_fusion), channel_id=1, source_target_pairs={{1,0},{2,1},{3,2},{4,3},{5,4},{6,5},{7,6},{8,7},{9,8},{10,9},{11,1... | collective-permute-start | bytes 860168 | tf_op jit(solution)/shard_map/ppermute | solution.py:29
  20.3 176.5 %collective-permute-start.2 = (f32[36,8192]{1,0:T(8,128)}, f32[36,8192]{1,0:T(8,128)}, u32[]{:S(2)}, u32[]{:S(2)}) collective-permute-start(f32[36,8192]{1,0:T(8,128)} %pad_maximum_fusion.1), channel_id=1, source_target_pairs={{0,1},{1,2},{2,3},{3,4},{4,5},{5,6},{6,7},{7,8},{8,9},{9,10},{10,1... | collective-permute-start | bytes 3538952 | tf_op jit(solution)/shard_map/ppermute | solution.py:28
  22.0 177.2 %collective-permute-start.3 = (f32[36,8192]{1,0:T(8,128)}, f32[36,8192]{1,0:T(8,128)}, u32[]{:S(2)}, u32[]{:S(2)}) collective-permute-start(f32[36,8192]{1,0:T(8,128)} %pad_maximum_fusion.1), channel_id=1, source_target_pairs={{1,0},{2,1},{3,2},{4,3},{5,4},{6,5},{7,6},{8,7},{9,8},{10,9},{11,1... | collective-permute-start | bytes 3538952 | tf_op jit(solution)/shard_map/ppermute | solution.py:29
  32.1 635.6 %all-gather.3.cloned.1.call-start = ((), (), s32[]{:S(2)}) async-start(), calls=%async_computation.1 | async-start | bytes 2641920 | tf_op jit(solution)/shard_map/all_gather | solution.py:73
  229.3 11.6 %copy-start.11 = (s32[32,27]{0,1:T(8,128)S(1)}, s32[32,27]{0,1:T(8,128)}, u32[]{:S(2)}) copy-start(s32[32,27]{0,1:T(8,128)} %copy-done.10) | copy-start | bytes 10372 | tf_op jit(solution)/shard_map/while
  246.4 11.6 %copy-start.11 = (s32[32,27]{0,1:T(8,128)S(1)}, s32[32,27]{0,1:T(8,128)}, u32[]{:S(2)}) copy-start(s32[32,27]{0,1:T(8,128)} %copy-done.10) | copy-start | bytes 10372 | tf_op jit(solution)/shard_map/while
  263.5 11.6 %copy-start.11 = (s32[32,27]{0,1:T(8,128)S(1)}, s32[32,27]{0,1:T(8,128)}, u32[]{:S(2)}) copy-start(s32[32,27]{0,1:T(8,128)} %copy-done.10) | copy-start | bytes 10372 | tf_op jit(solution)/shard_map/while
  280.5 11.6 %copy-start.11 = (s32[32,27]{0,1:T(8,128)S(1)}, s32[32,27]{0,1:T(8,128)}, u32[]{:S(2)}) copy-start(s32[32,27]{0,1:T(8,128)} %copy-done.10) | copy-start | bytes 10372 | tf_op jit(solution)/shard_map/while
  297.6 11.6 %copy-start.11 = (s32[32,27]{0,1:T(8,128)S(1)}, s32[32,27]{0,1:T(8,128)}, u32[]{:S(2)}) copy-start(s32[32,27]{0,1:T(8,128)} %copy-done.10) | copy-start | bytes 10372 | tf_op jit(solution)/shard_map/while
  314.7 11.6 %copy-start.11 = (s32[32,27]{0,1:T(8,128)S(1)}, s32[32,27]{0,1:T(8,128)}, u32[]{:S(2)}) copy-start(s32[32,27]{0,1:T(8,128)} %copy-done.10) | copy-start | bytes 10372 | tf_op jit(solution)/shard_map/while
  331.7 11.6 %copy-start.11 = (s32[32,27]{0,1:T(8,128)S(1)}, s32[32,27]{0,1:T(8,128)}, u32[]{:S(2)}) copy-start(s32[32,27]{0,1:T(8,128)} %copy-done.10) | copy-start | bytes 10372 | tf_op jit(solution)/shard_map/while
  348.8 11.6 %copy-start.11 = (s32[32,27]{0,1:T(8,128)S(1)}, s32[32,27]{0,1:T(8,128)}, u32[]{:S(2)}) copy-start(s32[32,27]{0,1:T(8,128)} %copy-done.10) | copy-start | bytes 10372 | tf_op jit(solution)/shard_map/while
  365.9 11.6 %copy-start.11 = (s32[32,27]{0,1:T(8,128)S(1)}, s32[32,27]{0,1:T(8,128)}, u32[]{:S(2)}) copy-start(s32[32,27]{0,1:T(8,128)} %copy-done.10) | copy-start | bytes 10372 | tf_op jit(solution)/shard_map/while
  382.9 11.6 %copy-start.11 = (s32[32,27]{0,1:T(8,128)S(1)}, s32[32,27]{0,1:T(8,128)}, u32[]{:S(2)}) copy-start(s32[32,27]{0,1:T(8,128)} %copy-done.10) | copy-start | bytes 10372 | tf_op jit(solution)/shard_map/while
  400.0 11.6 %copy-start.11 = (s32[32,27]{0,1:T(8,128)S(1)}, s32[32,27]{0,1:T(8,128)}, u32[]{:S(2)}) copy-start(s32[32,27]{0,1:T(8,128)} %copy-done.10) | copy-start | bytes 10372 | tf_op jit(solution)/shard_map/while
  417.1 11.6 %copy-start.11 = (s32[32,27]{0,1:T(8,128)S(1)}, s32[32,27]{0,1:T(8,128)}, u32[]{:S(2)}) copy-start(s32[32,27]{0,1:T(8,128)} %copy-done.10) | copy-start | bytes 10372 | tf_op jit(solution)/shard_map/while
  434.2 11.6 %copy-start.11 = (s32[32,27]{0,1:T(8,128)S(1)}, s32[32,27]{0,1:T(8,128)}, u32[]{:S(2)}) copy-start(s32[32,27]{0,1:T(8,128)} %copy-done.10) | copy-start | bytes 10372 | tf_op jit(solution)/shard_map/while
  451.2 11.6 %copy-start.11 = (s32[32,27]{0,1:T(8,128)S(1)}, s32[32,27]{0,1:T(8,128)}, u32[]{:S(2)}) copy-start(s32[32,27]{0,1:T(8,128)} %copy-done.10) | copy-start | bytes 10372 | tf_op jit(solution)/shard_map/while
  468.3 11.6 %copy-start.11 = (s32[32,27]{0,1:T(8,128)S(1)}, s32[32,27]{0,1:T(8,128)}, u32[]{:S(2)}) copy-start(s32[32,27]{0,1:T(8,128)} %copy-done.10) | copy-start | bytes 10372 | tf_op jit(solution)/shard_map/while
  485.4 11.6 %copy-start.11 = (s32[32,27]{0,1:T(8,128)S(1)}, s32[32,27]{0,1:T(8,128)}, u32[]{:S(2)}) copy-start(s32[32,27]{0,1:T(8,128)} %copy-done.10) | copy-start | bytes 10372 | tf_op jit(solution)/shard_map/while
  502.4 11.6 %copy-start.11 = (s32[32,27]{0,1:T(8,128)S(1)}, s32[32,27]{0,1:T(8,128)}, u32[]{:S(2)}) copy-start(s32[32,27]{0,1:T(8,128)} %copy-done.10) | copy-start | bytes 10372 | tf_op jit(solution)/shard_map/while
  519.5 11.6 %copy-start.11 = (s32[32,27]{0,1:T(8,128)S(1)}, s32[32,27]{0,1:T(8,128)}, u32[]{:S(2)}) copy-start(s32[32,27]{0,1:T(8,128)} %copy-done.10) | copy-start | bytes 10372 | tf_op jit(solution)/shard_map/while
  536.6 11.6 %copy-start.11 = (s32[32,27]{0,1:T(8,128)S(1)}, s32[32,27]{0,1:T(8,128)}, u32[]{:S(2)}) copy-start(s32[32,27]{0,1:T(8,128)} %copy-done.10) | copy-start | bytes 10372 | tf_op jit(solution)/shard_map/while
  553.6 11.6 %copy-start.11 = (s32[32,27]{0,1:T(8,128)S(1)}, s32[32,27]{0,1:T(8,128)}, u32[]{:S(2)}) copy-start(s32[32,27]{0,1:T(8,128)} %copy-done.10) | copy-start | bytes 10372 | tf_op jit(solution)/shard_map/while
  570.7 11.6 %copy-start.11 = (s32[32,27]{0,1:T(8,128)S(1)}, s32[32,27]{0,1:T(8,128)}, u32[]{:S(2)}) copy-start(s32[32,27]{0,1:T(8,128)} %copy-done.10) | copy-start | bytes 10372 | tf_op jit(solution)/shard_map/while
  604.9 11.6 %copy-start.11 = (s32[32,27]{0,1:T(8,128)S(1)}, s32[32,27]{0,1:T(8,128)}, u32[]{:S(2)}) copy-start(s32[32,27]{0,1:T(8,128)} %copy-done.10) | copy-start | bytes 10372 | tf_op jit(solution)/shard_map/while
  621.9 11.6 %copy-start.11 = (s32[32,27]{0,1:T(8,128)S(1)}, s32[32,27]{0,1:T(8,128)}, u32[]{:S(2)}) copy-start(s32[32,27]{0,1:T(8,128)} %copy-done.10) | copy-start | bytes 10372 | tf_op jit(solution)/shard_map/while
  677.2 29.1 %copy-start.7 = (f32[32,32,256]{2,0,1:T(8,128)S(1)}, f32[32,32,256]{2,0,1:T(8,128)}, u32[]{:S(2)}) copy-start(f32[32,32,256]{2,0,1:T(8,128)} %get-tuple-element.114) | copy-start | bytes 3145732
  (66 other events, 129.9 us)
Sparse Core Ops, SparseCore 0:
  32.2 139.9 all-reduce.1
  175.9 63.3 all-gather.2
where the time goes:
time: 718 us; the launch traced here: 715 us
  matrix products  354 us (49%)
  local copies, waits for them, and re-layouts  167 us (23%)
  waiting for transfers between devices  128 us (18%)
  other arithmetic  40.3 us (6%)
  between operations  13.7 us (2%)
  starting transfers between devices  9.85 us (1%)
    dot_general x27, matrix products, slot(): jnp.einsum('rlb,lba->rla', picked[:NRHS], block_kernel, precision=highest)  313 us
    psum x1, waiting for transfers between devices, shards(): top_coef = lax.psum(placed, 'clus')  128 us
    gather x27, local copies, waits for them, and re-layouts, slot(): picked = jnp.take(point_window, chosen, axis=1)  74 us
    while x189, local copies, waits for them, and re-layouts  44.5 us
    dot_general x1, matrix products, shards(): jnp.einsum('rlfj,lfji->rli', far_picked[:NRHS], coupling, precision=highest)  29.1 us
    convert_element_type x27, other arithmetic, slot(): live = (index < near_count).astype(jnp.float32)  17.8 us
  transfers between devices with their start and end apart: 6, of which 1 were waited for; matrix products, arithmetic and copies ran while one was open for 65% of the time, Pallas kernels for 0%

commit v1 on v0

v1 whole, which is shorter than its diff:
```python
import functools
import math

import jax
import jax.numpy as jnp
from jax import lax
from jax.experimental import pallas as pl
from jax.experimental.pallas import tpu as pltpu
from jax.sharding import PartitionSpec as P

LEAF = 256
RANK = 64
NRHS = 32
LEAF_DEV = 32
NEAR_MAX = 27
FAR2 = 16
GROUP = 8

STEP = 4
LIST = 1024
FEAT = 64
UNROLL = 4

smoothing = 0.05
inv_four_pi = 1.0 / (4.0 * math.pi)
highest = lax.Precision.HIGHEST
bf16 = jnp.bfloat16
f32 = jnp.float32
NN = (((1,), (0,)), ((), ()))
NT = (((1,), (1,)), ((), ()))
SMEM = pl.BlockSpec(memory_space=pltpu.SMEM)
VMEM = pl.BlockSpec(memory_space=pltpu.VMEM)


def product(left, right, dims, precision=None):
    return lax.dot_general(left, right, dims, precision=precision, preferred_element_type=f32)


def green(source, target):
    first = source[0][..., :, None] - target[0][..., None, :]
    second = source[1][..., :, None] - target[1][..., None, :]
    third = source[2][..., :, None] - target[2][..., None, :]
    total = first * first + second * second + third * third
    return inv_four_pi / jnp.sqrt(total + smoothing * smoothing)


def source_rows(out, points):
    width = points.shape[1]
    out[0:3] = points
    out[3:4] = jnp.sum(points * points, axis=0, keepdims=True)
    out[4:5] = jnp.ones((1, width), f32)
    out[5:8] = jnp.zeros((3, width), f32)


def target_rows(out, points):
    width = points.shape[1]
    out[0:3] = points * -2.0
    out[3:4] = jnp.ones((1, width), f32)
    out[4:5] = jnp.sum(points * points, axis=0, keepdims=True) + smoothing * smoothing
    out[5:8] = jnp.zeros((3, width), f32)


def three(rows):
    first = rows.astype(bf16).astype(f32)
    rest = rows - first
    second = rest.astype(bf16).astype(f32)
    third = (rest - second).astype(bf16).astype(f32)
    return first, second, third


def source_features(rows):
    a, b, c = three(rows)
    return jnp.concatenate([a, a, b, a, c, b, b, c], axis=0)


def target_features(rows):
    a, b, c = three(rows)
    return jnp.concatenate([a, b, a, c, a, b, c, b], axis=0)


def two(values):
    high = values.astype(bf16)
    low = (values - high.astype(f32)).astype(bf16)
    return high, low


def upward_kernel(
    code_ref,
    charges_ref,
    points_ref,
    weights_ref,
    basis_ref,
    nodes_ref,
    transfer_ref,
    mid_nodes_ref,
    mid_transfer_ref,
    pack_ref,
    target_ref,
    coef_ref,
    node_target_ref,
    level_ref,
    list_ref,
    total,
    counts,
):
    step = pl.program_id(0)

    @pl.when(step == 0)
    def _():
        total[...] = jnp.zeros_like(total)
        counts[0] = 0

    charges = charges_ref[...]
    points = points_ref[...]
    pack_ref[0:NRHS] = charges * (weights_ref[...] * inv_four_pi)
    source_rows(pack_ref.at[NRHS : NRHS + 8], points)
    target_rows(target_ref, points)
    for leaf in range(STEP):
        own = charges[:, leaf * LEAF : (leaf + 1) * LEAF]
        coef = product(own, basis_ref[leaf], NT, highest)
        coef_ref[0:NRHS, leaf * RANK : (leaf + 1) * RANK] = coef
    source_rows(coef_ref.at[NRHS : NRHS + 8], nodes_ref[...])
    target_rows(node_target_ref, nodes_ref[...])
    total[...] += product(coef_ref[0:NRHS], transfer_ref[...], NT, highest)

    count = counts[0]
    for slot in range(STEP * NEAR_MAX):
        code = code_ref[step * (STEP * NEAR_MAX) + slot]
        shift = lax.shift_right_logical(code, 12) & 31
        place = lax.shift_right_logical(count, shift) & (LIST - 1)
        list_ref[lax.shift_left(lax.shift_right_logical(code, 17), 10) + place] = code
        count = count + lax.shift_left(1, shift)
    counts[0] = count

    @pl.when(step == pl.num_programs(0) - 1)
    def _():
        mid_coef = total[...]
        level_ref[0:NRHS] = mid_coef
        level_ref[NRHS : 2 * NRHS] = product(mid_coef, mid_transfer_ref[...], NT, highest)
        source_rows(level_ref.at[2 * NRHS : 2 * NRHS + 8], mid_nodes_ref[...])
        for phase in range(3):
            number = lax.shift_right_logical(count, 10 * phase) & (LIST - 1)
            for spare in range(8):
                list_ref[phase * LIST + number + spare] = LEAF_DEV * 64
            list_ref[phase * LIST + LIST - 1] = number


def upward(codes, charges, points, weights, basis, nodes, transfer, mid_nodes, mid_transfer):
    lanes = lambda rows, width: pl.BlockSpec((rows, width), lambda i: (0, i))
    fixed = lambda rows, width: pl.BlockSpec((rows, width), lambda i: (0, 0))
    wide, narrow = STEP * LEAF, STEP * RANK
    shape = jax.ShapeDtypeStruct
    return pl.pallas_call(
        upward_kernel,
        grid=(LEAF_DEV // STEP,),
        in_specs=[
            SMEM,
            lanes(NRHS, wide),
            lanes(3, wide),
            lanes(1, wide),
            pl.BlockSpec((STEP, RANK, LEAF), lambda i: (i, 0, 0)),
            lanes(3, narrow),
            lanes(RANK, narrow),
            fixed(3, RANK),
            fixed(RANK, RANK),
        ],
        out_specs=[
            lanes(NRHS + 8, wide),
            lanes(8, wide),
            lanes(NRHS + 8, narrow),
            lanes(8, narrow),
            fixed(2 * NRHS + 8, RANK),
            SMEM,
        ],
        out_shape=[
            shape((NRHS + 8, LEAF_DEV * LEAF), f32),
            shape((8, LEAF_DEV * LEAF), f32),
            shape((NRHS + 8, LEAF_DEV * RANK), f32),
            shape((8, LEAF_DEV * RANK), f32),
            shape((2 * NRHS + 8, RANK), f32),
            shape((4 * LIST,), jnp.int32),
        ],
        scratch_shapes=[pltpu.VMEM((NRHS, RANK), f32), pltpu.SMEM((1,), jnp.int32)],
        name="upward",
    )(codes, charges, points, weights, basis, nodes, transfer, mid_nodes, mid_transfer)


def near_kernel(phase, list_ref, pack_ref, target_ref, *refs):
    if phase == 0:
        (out_ref, source, target, sides, squares, highs, lows) = refs
        out_ref[...] = jnp.zeros_like(out_ref)
    else:
        (before_ref, out_ref, source, target, sides, squares, highs, lows) = refs
        out_ref[...] = before_ref[...]

    def prepare(leaf, _):
        start = pl.multiple_of(leaf * LEAF, LEAF)
        features = source_features(pack_ref[NRHS : NRHS + 8, pl.ds(start, LEAF)])
        source[leaf] = features.T.astype(bf16)
        target[leaf] = target_features(target_ref[:, pl.ds(start, LEAF)]).astype(bf16)
        high, low = two(pack_ref[0:NRHS, pl.ds(start, LEAF)])
        sides[leaf, 0:NRHS] = high
        sides[leaf, NRHS : 2 * NRHS] = low
        return 0

    lax.fori_loop(0, LEAF_DEV, prepare, 0)

    def item(index):
        code = list_ref[phase * LIST + index]
        return lax.shift_right_logical(code, 6) & 63, code & 63

    def distances(index, slot):
        to, of = item(index)
        squares[slot] = product(source[of], target[to], NN)

    def values(slot):
        for row in range(0, LEAF, 64):
            high, low = two(lax.rsqrt(squares[slot, row : row + 64]))
            highs[slot, row : row + 64] = high
            lows[slot, row : row + 64] = low

    def apply(index, slot):
        to, of = item(index)
        upper = product(sides[of], highs[slot], NN)
        lower = product(sides[of, 0:NRHS], lows[slot], NN)
        out_ref[to] += upper[0:NRHS] + upper[NRHS : 2 * NRHS] + lower

    distances(0, 0)
    distances(1, 1)
    values(0)

    def step(number, _):
        for part in range(UNROLL):
            index = number * UNROLL + part
            apply(index, part % 2)
            values((part + 1) % 2)
            distances(index + 2, part % 2)
        return 0

    length = list_ref[phase * LIST + LIST - 1]
    lax.fori_loop(0, lax.div(length + (UNROLL - 1), UNROLL), step, 0)


def near(phase, lists, pack, targets, before):
    operands = (lists, pack, targets) + (() if before is None else (before,))
    rows = LEAF_DEV + 1
    return pl.pallas_call(
        functools.partial(near_kernel, phase),
        in_specs=[SMEM] + [VMEM] * (len(operands) - 1),
        out_specs=VMEM,
        out_shape=jax.ShapeDtypeStruct((rows, NRHS, LEAF), f32),
        scratch_shapes=[
            pltpu.VMEM((LEAF_DEV, LEAF, FEAT), bf16),
            pltpu.VMEM((rows, FEAT, LEAF), bf16),
            pltpu.VMEM((LEAF_DEV, 2 * NRHS, LEAF), bf16),
            pltpu.VMEM((2, LEAF, LEAF), f32),
            pltpu.VMEM((2, LEAF, LEAF), bf16),
            pltpu.VMEM((2, LEAF, LEAF), bf16),
        ],
        compiler_params=pltpu.CompilerParams(vmem_limit_bytes=40 * 2**20),
        cost_estimate=pl.CostEstimate(flops=20_000_000_000, bytes_accessed=4_000_000, transcendentals=14_000_000),
        name="near" + str(phase),
    )(*operands)


def final_kernel(near_ref, field_ref, basis_ref, out_ref):
    for leaf in range(STEP):
        field = field_ref[:, leaf * RANK : (leaf + 1) * RANK]
        far = product(field, basis_ref[leaf], NN, highest)
        out_ref[:, leaf * LEAF : (leaf + 1) * LEAF] = far + near_ref[leaf]


def final(near_out, field, basis):
    return pl.pallas_call(
        final_kernel,
        grid=(LEAF_DEV // STEP,),
        in_specs=[
            pl.BlockSpec((STEP, NRHS, LEAF), lambda i: (i, 0, 0)),
            pl.BlockSpec((NRHS, STEP * RANK), lambda i: (0, i)),
            pl.BlockSpec((STEP, RANK, LEAF), lambda i: (i, 0, 0)),
        ],
        out_specs=pl.BlockSpec((NRHS, STEP * LEAF), lambda i: (0, i)),
        out_shape=jax.ShapeDtypeStruct((NRHS, LEAF_DEV * LEAF), f32),
        name="final",
    )(near_out, field, basis)


def shards(
    charges,
    positions,
    quad_weights,
    leaf_basis,
    leaf_nodes,
    leaf_transfer,
    mid_nodes,
    mid_transfer,
    top_nodes,
    near_list,
    near_count,
    far_list,
    mid_mask,
    top_mask,
):
    devices = lax.axis_size("clus")
    myself = lax.axis_index("clus")
    top_count = devices // GROUP
    partner = [(i, i ^ 1) for i in range(devices)]
    cross = [(i, (i + 1 if i % 2 else i - 1) % devices) for i in range(devices)]
    partner_step = jnp.where(myself % 2 == 0, 1, devices - 1)

    def phase_of(leaves):
        away = (leaves // LEAF_DEV - myself) % devices
        return jnp.where(away == 0, 0, jnp.where(away == partner_step, 1, 2))

    live = jnp.arange(NEAR_MAX)[None, :] < near_count[:, None]
    phase = jnp.where(live, phase_of(near_list), 3)
    leaf_row = jnp.arange(LEAF_DEV, dtype=jnp.int32)[:, None]
    codes = (phase << 17) | ((10 * phase) << 12) | (leaf_row << 6) | (near_list % LEAF_DEV)

    pack, targets, coef, node_targets, level, lists = upward(
        codes.reshape(-1).astype(jnp.int32),
        charges,
        positions,
        quad_weights.reshape(1, -1),
        leaf_basis,
        leaf_nodes,
        leaf_transfer,
        mid_nodes,
        mid_transfer,
    )
    pack_partner = lax.ppermute(pack, "clus", partner)
    coef_partner = lax.ppermute(coef, "clus", partner)
    pack_cross = lax.ppermute(pack, "clus", cross)
    coef_cross = lax.ppermute(coef, "clus", cross)
    everyone = lax.all_gather(level, "clus", axis=0, tiled=False)

    near_out = near(0, lists, pack, targets, None)
    near_out = near(1, lists, pack_partner, targets, near_out)
    near_out = near(2, lists, pack_cross, targets, near_out)

    flat = jnp.transpose(everyone, (1, 0, 2)).reshape(2 * NRHS + 8, devices * RANK)
    all_coef = flat[:NRHS]
    all_nodes = flat[2 * NRHS : 2 * NRHS + 3]
    upward_sum = everyone[:, NRHS : 2 * NRHS].reshape(top_count, GROUP, NRHS, RANK).sum(axis=1)
    top_coef = jnp.transpose(upward_sum, (1, 0, 2)).reshape(NRHS, top_count * RANK)
    parent = myself // GROUP
    top_target = lax.dynamic_slice_in_dim(top_nodes, parent * RANK, RANK, 1)
    top_row = lax.dynamic_index_in_dim(top_mask, parent, 0, keepdims=False)
    top_select = jnp.repeat(top_row.astype(f32), RANK)[:, None]
    top_field = jnp.dot(top_coef, green(top_nodes, top_target) * top_select, precision=highest)
    mid_select = jnp.repeat(mid_mask[0].astype(f32), RANK)[:, None]
    mid_field = jnp.dot(all_coef, green(all_nodes, mid_nodes) * mid_select, precision=highest)
    mid_field = mid_field + jnp.dot(top_field, mid_transfer, precision=highest)
    leaf_down = jnp.dot(mid_field, leaf_transfer, precision=highest).reshape(NRHS, LEAF_DEV, RANK)

    window = jnp.concatenate([coef, coef_partner, coef_cross], axis=1)
    window = window.reshape(NRHS + 8, 3 * LEAF_DEV, RANK)
    far_local = phase_of(far_list) * LEAF_DEV + far_list % LEAF_DEV
    picked = jnp.take(window, far_local, axis=1)
    target_nodes = leaf_nodes.reshape(3, LEAF_DEV, RANK)
    coupling = green(picked[NRHS : NRHS + 3], target_nodes[:, :, None, :])
    field = jnp.einsum("rlfj,lfji->rli", picked[:NRHS], coupling, precision=highest) + leaf_down
    return final(near_out, field.reshape(NRHS, LEAF_DEV * RANK), leaf_basis)


def solution(mesh):
    in_specs = (
        P(None, "clus"),
        P(None, "clus"),
        P("clus"),
        P("clus", None, None),
        P(None, "clus"),
        P(None, "clus"),
        P(None, "clus"),
        P(None, "clus"),
        P(),
        P("clus", None),
        P("clus"),
        P("clus", None),
        P("clus", None),
        P(),
    )
    out_specs = P(None, "clus")
    return jax.shard_map(shards, mesh=mesh, in_specs=in_specs, out_specs=out_specs, check_vma=False)
```

time: 718 us -> 216 us (0.30)
  the two profiles are of different devices: /device:TPU:1 before, /device:TPU:25 now
where the time goes in v1:
time: 216 us; the launch traced here: 217 us
  Pallas kernels  107 us (50%)
  local copies, waits for them, and re-layouts  40.7 us (19%)
  matrix products  38.3 us (18%)
  between operations  13.6 us (6%)
  other arithmetic  10 us (5%)
  starting transfers between devices  7.55 us (3%)
    pallas_call x3, Pallas kernels, near(): pl.pallas_call(functools.partial(near_kernel, phase), in_specs=[SMEM] + [...  91 us
    dot_general x1, matrix products, shards(): jnp.einsum('rlfj,lfji->rli', picked[:NRHS], coupling, precision=highest)  27.7 us
    slice x4, local copies, waits for them, and re-layouts, green(): first = source[0][..., :, None] - target[0][..., None, :]  13 us
    unnamed x31, local copies, waits for them, and re-layouts  9.86 us
    pallas_call x1, Pallas kernels, upward(): pl.pallas_call(upward_kernel, grid=(LEAF_DEV // STEP,), in_specs=[SMEM, l...  9.31 us
    dot_general x1, matrix products, shards(): jnp.dot(all_coef, green(all_nodes, mid_nodes) * mid_select, precision=hig...  9.03 us
    reshape x2, local copies, waits for them, and re-layouts, shards(): window = window.reshape(NRHS + 8, 3 * LEAF_DEV, RANK)  7.04 us
    pallas_call x1, Pallas kernels, final(): pl.pallas_call(final_kernel, grid=(LEAF_DEV // STEP,), in_specs=[pl.Block...  6.84 us
  transfers between devices with their start and end apart: 5, of which 0 were waited for; matrix products, arithmetic and copies ran while one was open for 12% of the time, Pallas kernels for 42%

profile of v1, /device:TPU:25, one launch (start us, length us, event | category | flops | bytes accessed | tf_op | source)
XLA Modules:
  0.0 217.3 jit_solution(1887021842546960839)
XLA Ops:
  6.6 0.8 fusion.73
  7.4 0.7 reshape.71.code_ref
  8.1 9.3 %upward.1 = (f32[40,8192]{1,0:T(8,128)}, f32[8,8192]{1,0:T(8,128)}, f32[40,2048]{1,0:T(8,128)}, f32[8,2048]{1,0:T(8,128)}, f32[72,64]{1,0:T(8,128)}, /*index=5*/s32[4096]{0:T(1024)}) custom-call(s32[864]{0:T(1024)} %reshape.71.code_ref, f32[32,8192]{1,0:T(8,128)} %charges_ref.1, f32[3,8192]{1,0:T(4,128)} %points_ref.1, f32[1,8192]{1,0:T(1,128)} %bitcast.59, ...), custom_call_target="tpu_custom_call" | custom-call | tf_op jit(solution)/shard_map/upward/pallas_call | solution.py:153
  17.4 1.9 collective-permute-start
  19.2 4.8 %collective-permute-start.1 = (f32[40,8192]{1,0:T(8,128)}, f32[40,8192]{1,0:T(8,128)S(1)}, u32[]{:S(2)}, u32[]{:S(2)}) collective-permute-start(f32[40,8192]{1,0:T(8,128)} %get-tuple-element.11.pack_ref), channel_id=1, source_target_pairs={{0,1},{1,0},{2,3},{3,2},{4,5},{5,4},{6,7},{7,6},{8,9},{9,8},{10,11... | collective-permute-start | bytes 3932168 | tf_op jit(solution)/shard_map/ppermute | solution.py:331
  24.0 0.9 collective-permute-start.2
  24.9 1.5 copy.45
  26.4 0.9 slice_reduce_fusion.5
  27.3 0.8 slice_bitcast_fusion.5
  28.1 0.7 compare_and_fusion
  29.5 0.7 multiply_bitcast_fusion
  30.4 1.3 copy-done.1
  31.8 0.9 copy-done.2
  32.7 0.7 copy-done.4
  33.4 31.4 %near0.1.refs_0_ = f32[33,32,256]{2,1,0:T(8,128)S(1)} custom-call(s32[4096]{0:T(1024)S(1)} %copy-done.4, f32[40,8192]{1,0:T(8,128)S(1)} %copy-done.1, f32[8,8192]{1,0:T(8,128)S(1)} %copy-done.2), custom_call_target="tpu_custom_call" | custom-call | flops 20000000000 | bytes 4000000 | tf_op jit(solution)/shard_map/near0/pallas_call | solution.py:247
  64.8 1.0 copy-done.6
  65.8 1.0 pad_maximum_fusion
  66.9 3.1 %reshape.73 = f32[40,96,64]{2,1,0:T(8,128)} reshape(f32[40,6144]{1,0:T(8,128)} %pad_maximum_fusion) | data formatting | bytes 1966080 | tf_op jit(solution)/shard_map/reshape | solution.py:357
  69.9 4.0 %copy.44 = f32[40,96,64]{2,0,1:T(8,128)} copy(f32[40,96,64]{2,1,0:T(8,128)} %reshape.73) | data formatting | bytes 1966080 | tf_op jit(solution)/shard_map/reshape | solution.py:357
  73.9 6.8 %gather_fusion = f32[512,40,64]{2,1,0:T(8,128)} fusion(f32[40,96,64]{2,0,1:T(8,128)} %copy.44, s32[1024]{0:T(1024)S(1)} %pad_clamp_fusion), kind=kCustom, calls=%fused_computation | custom fusion | bytes 10487808 | tf_op jit(solution)/shard_map/jit(_take)/gather | solution.py:359
  80.7 5.4 %select_bitcast_fusion = f32[40,32,16,64]{3,0,2,1:T(8,128)S(1)} fusion(f32[32,16,40,64]{3,2,1,0:T(8,128)} %bitcast.53, pred[32,16]{1,0:T(8,128)(4,1)S(1)} %copy.42), kind=kLoop, calls=%fused_computation.13 | loop fusion | flops 1310720 | bytes 10486272 | tf_op jit(solution)/shard_map/jit(_take)/select_n | solution.py:359
  86.7 3.4 %copy-done.9 = f32[40,32,16,64]{3,0,2,1:T(8,128)} copy-done((f32[40,32,16,64]{3,0,2,1:T(8,128)}, f32[40,32,16,64]{3,0,2,1:T(8,128)S(1)}, u32[]{:S(2)}) %copy-start.9) | copy-done | bytes 5242904
  90.1 29.9 %near1.1.refs_0_ = f32[33,32,256]{2,1,0:T(8,128)S(1)} custom-call(s32[4096]{0:T(1024)S(1)} %copy-done.5, f32[40,8192]{1,0:T(8,128)S(1)} %collective-permute-done.1.pack_ref, f32[8,8192]{1,0:T(8,128)S(1)} %copy-done.3, f32[33,32,256]{2,1,0:T(8,128)S(1)} %copy-done.7), custom_call_target="tpu_custom_call" | custom-call | flops 20000000000 | bytes 4000000 | tf_op jit(solution)/shard_map/near1/pallas_call | solution.py:247
  120.1 29.7 %near2.1.near_ref = f32[33,32,256]{2,1,0:T(8,128)S(1)} custom-call(s32[4096]{0:T(1024)S(1)} %copy-done.5, f32[40,8192]{1,0:T(8,128)S(1)} %collective-permute-done.pack_ref, f32[8,8192]{1,0:T(8,128)S(1)} %copy-done.3, f32[33,32,256]{2,1,0:T(8,128)S(1)} %near1.1.refs_0_), custom_call_target="tpu_custom_call" | custom-call | flops 20000000000 | bytes 4000000 | tf_op jit(solution)/shard_map/near2/pallas_call | solution.py:247
  149.8 1.0 copy-done
  150.8 11.5 %slice_reduce_fusion.2 = (f32[128,64]{1,0:T(8,128)S(1)}, f32[128,64]{1,0:T(8,128)S(1)}, f32[128,64]{1,0:T(8,128)S(1)}) fusion(f32[72,128,64]{0,2,1:T(8,128)} %bitcast.51), kind=kLoop, calls=%fused_computation.25 | loop fusion | bytes 196608 | tf_op jit(solution)/shard_map/slice | solution.py:40
  162.5 9.0 %fusion.21 = f32[32,64]{1,0:T(8,128)S(1)} fusion(f32[32,8192]{0,1:T(8,128)} %bitcast.52, f32[8192]{0:T(1024)S(1)} %mul.84, f32[64]{0:T(128)S(1)} %get-tuple-element.33, f32[8192]{0:T(1024)S(1)} %sub.212, f32[64]{0:T(128)S(1)} %get-tuple-element.34, f32[8192]{0:T(1024)S(1)} %sub.207, f32[64]{0:T(128)S(1)} %get-tuple-element.32, f32[8192]{0:T(1024)S(1)} %sub.202), kind=kOutput, calls=%fused_computation.27 | convolution fusion | flops 206569472 | bytes 1188608 | tf_op jit(solution)/shard_map/dot_general | solution.py:352
  171.6 1.4 bitcast_reduce_fusion
  172.9 1.0 fusion.51
  174.8 27.7 %fusion.38 = f32[32,32,64]{2,0,1:T(8,128)S(1)} fusion(f32[40,32,16,64]{3,0,2,1:T(8,128)} %copy-done.9, f32[32,64]{1,0:T(8,128)S(1)} %sub.199, f32[32,16,64]{2,1,0:T(8,128)S(1)} %bitcast.56, f32[32,64]{1,0:T(8,128)S(1)} %sub.194, f32[32,16,64]{2,1,0:T(8,128)S(1)} %bitcast.57, f32[32,64]{1,0:T(8,128)S(1)} %sub.189, f32[32,16,64]{2,1,0:T(8,128)S(1)} %bitcast.55, ...), kind=kOutput, calls=%fused_computation.40 | convolution fusion | flops 826343424 | bytes 9330688 | tf_op jit(solution)/shard_map/rlfj,lfji->rli/dot_general | solution.py:362
  202.8 0.9 reshape.77.field_ref
  203.6 6.8 %final.1 = f32[32,8192]{1,0:T(8,128)} custom-call(f32[33,32,256]{2,1,0:T(8,128)} %copy-done, f32[32,2048]{1,0:T(8,128)} %reshape.77.field_ref, f32[32,64,256]{2,1,0:T(8,128)} %basis_ref.3), custom_call_target="tpu_custom_call" | custom-call | tf_op jit(solution)/shard_map/final/pallas_call | solution.py:274
  (56 shorter events, 2.8 us)
Async XLA Ops:
  6.5 22.8 %copy-start.14 = (s32[1,128]{1,0:T(1,128)S(1)}, s32[1,128]{1,0:T(1,128)}, u32[]{:S(2)}) copy-start(s32[1,128]{1,0:T(1,128)} %param.26) | copy-start | bytes 1540
  6.5 23.8 %copy-start.13 = (f32[3,1024]{1,0:T(4,128)S(1)}, f32[3,1024]{1,0:T(4,128)}, u32[]{:S(2)}) copy-start(f32[3,1024]{1,0:T(4,128)} %param.22) | copy-start | bytes 36868
  6.5 144.2 %all-gather.4.cloned.1.call-start = ((), (), s32[]{:S(2)}) async-start(), calls=%async_computation | async-start | bytes 4227072 | tf_op jit(solution)/shard_map/all_gather | solution.py:335
  17.4 102.7 %collective-permute-start = (f32[40,8192]{1,0:T(8,128)}, f32[40,8192]{1,0:T(8,128)S(1)}, u32[]{:S(2)}, u32[]{:S(2)}) collective-permute-start(f32[40,8192]{1,0:T(8,128)} %get-tuple-element.11.pack_ref), channel_id=1, source_target_pairs={{0,127},{1,2},{2,1},{3,4},{4,3},{5,6},{6,5},{7,8},{8,7},{9,10},{10... | collective-permute-start | bytes 3932168 | tf_op jit(solution)/shard_map/ppermute | solution.py:333
  19.2 70.9 %collective-permute-start.1 = (f32[40,8192]{1,0:T(8,128)}, f32[40,8192]{1,0:T(8,128)S(1)}, u32[]{:S(2)}, u32[]{:S(2)}) collective-permute-start(f32[40,8192]{1,0:T(8,128)} %get-tuple-element.11.pack_ref), channel_id=1, source_target_pairs={{0,1},{1,0},{2,3},{3,2},{4,5},{5,4},{6,7},{7,6},{8,9},{9,8},{10,11... | collective-permute-start | bytes 3932168 | tf_op jit(solution)/shard_map/ppermute | solution.py:331
  24.0 41.8 %collective-permute-start.3 = (f32[40,2048]{1,0:T(8,128)}, f32[40,2048]{1,0:T(8,128)S(1)}, u32[]{:S(2)}, u32[]{:S(2)}) collective-permute-start(f32[40,2048]{1,0:T(8,128)} %get-tuple-element.13), channel_id=1, source_target_pairs={{0,127},{1,2},{2,1},{3,4},{4,3},{5,6},{6,5},{7,8},{8,7},{9,10},{10... | collective-permute-start | bytes 983048 | tf_op jit(solution)/shard_map/ppermute | solution.py:334
  24.0 41.9 %collective-permute-start.2 = (f32[40,2048]{1,0:T(8,128)}, f32[40,2048]{1,0:T(8,128)S(1)}, u32[]{:S(2)}, u32[]{:S(2)}) collective-permute-start(f32[40,2048]{1,0:T(8,128)} %get-tuple-element.13), channel_id=1, source_target_pairs={{0,1},{1,0},{2,3},{3,2},{4,5},{5,4},{6,7},{7,6},{8,9},{9,8},{10,11... | collective-permute-start | bytes 983048 | tf_op jit(solution)/shard_map/ppermute | solution.py:332
  30.4 1.3 copy-start.1
  31.7 0.9 copy-start.2
  32.7 0.7 copy-start.4
  33.4 32.4 %copy-start.11 = (f32[40,2048]{1,0:T(8,128)S(1)}, f32[40,2048]{1,0:T(8,128)}, u32[]{:S(2)}) copy-start(f32[40,2048]{1,0:T(8,128)} %get-tuple-element.13) | copy-start | bytes 983044
  64.8 1.0 copy-start.6
  80.7 9.4 %copy-start.3 = (f32[8,8192]{1,0:T(8,128)S(1)}, f32[8,8192]{1,0:T(8,128)}, u32[]{:S(2)}) copy-start(f32[8,8192]{1,0:T(8,128)} %get-tuple-element.12.target_ref) | copy-start | bytes 786436
  80.7 9.4 %copy-start.5 = (s32[4096]{0:T(1024)S(1)}, s32[4096]{0:T(1024)}, u32[]{:S(2)}) copy-start(s32[4096]{0:T(1024)} %get-tuple-element.10.list_ref) | copy-start | bytes 49156
  80.7 9.4 %copy-start.7 = (f32[33,32,256]{2,1,0:T(8,128)S(1)}, f32[33,32,256]{2,1,0:T(8,128)}, u32[]{:S(2)}) copy-start(f32[33,32,256]{2,1,0:T(8,128)} %copy-done.6) | copy-start | bytes 3244036
  86.1 4.0 %copy-start.9 = (f32[40,32,16,64]{3,0,2,1:T(8,128)}, f32[40,32,16,64]{3,0,2,1:T(8,128)S(1)}, u32[]{:S(2)}) copy-start(f32[40,32,16,64]{3,0,2,1:T(8,128)S(1)} %select_bitcast_fusion) | copy-start | bytes 15728644
  149.8 1.0 copy-start
  162.5 9.0 %copy-start.8 = (f32[128,72,64]{1,2,0:T(8,128)S(1)}, f32[128,72,64]{1,2,0:T(8,128)}, u32[]{:S(2)}) copy-start(f32[128,72,64]{1,2,0:T(8,128)} %all-gather.4.cloned.1.call-done) | copy-start | bytes 7077892
  171.6 2.4 %copy-start.12 = (f32[64,64]{1,0:T(8,128)S(1)}, f32[64,64]{1,0:T(8,128)}, u32[]{:S(2)}) copy-start(f32[64,64]{1,0:T(8,128)} %mid_transfer_ref.1) | copy-start | bytes 49156
  171.6 2.6 %copy-start.10 = (f32[64,2048]{1,0:T(8,128)S(1)}, f32[64,2048]{1,0:T(8,128)}, u32[]{:S(2)}) copy-start(f32[64,2048]{1,0:T(8,128)} %transfer_ref.1) | copy-start | bytes 1572868
Sparse Core Ops, SparseCore 0:
  26.5 66.8 all-gather.3
